TPU v7x, 32 devices: a whole 2x2x4 slice. The times are simulated.
32 devices in a mesh: cand: 8 (over y, x, core), row: 4 (over z).
Axes of the slice: x: 2, y: 2, z: 4, core: 2. Of those that a mesh axis runs over, the one named last changes fastest.
Arguments:
- right_side: bfloat16 [16384, 8192], P('row', 'cand'), may hold values from -6 to 6
- factor_panel: bfloat16 [4, 4096, 1024], P('row', 'cand'), may hold values from -6 to 6
- diag_inverse: float32 [2, 512, 512], replicated, as said below
- prior_variance: float32 [8192], P('cand'), may hold values from 12 to 20
- block_index: int32 [1], replicated, may hold values from 0 to 30
Outputs:
- solved_side: bfloat16 [16384, 8192], P('row', 'cand')
- variance: float32 [8192], P('cand')
Inputs may be any that keep to these rules, and one draw needn't show every extreme that they name: Each diag_inverse[s] is lower triangular with positive diagonal. Blocks block_index[0] .. block_index[0] + 1 lie inside the window.
All inputs are finite; a program needn't handle non-finite values.
Results may differ from a plain program's by a relative error of at most 0.0037.
Values may be sent and summed in bfloat16 or wider, within the bound.
A program may use at most 128 MiB of HBM per device.

v0:
```python
import jax
import jax.numpy as jnp
from jax import lax
from jax.sharding import PartitionSpec as P


def spread(value, axis, root):
    mine = lax.axis_index(axis) == root
    return lax.psum(jnp.where(mine, value, jnp.zeros_like(value)), axis)


def shards(right_side, factor_panel, diag_inverse, prior_variance, block_index):
    rows_dev = right_side.shape[0]
    steps_all = diag_inverse.shape[0]
    block_rows = diag_inverse.shape[1]
    blocks_dev = rows_dev // block_rows
    row_here = lax.axis_index("row")
    local_factor = factor_panel[0]
    working = right_side.astype(jnp.float32)
    global_block = (row_here * blocks_dev + jnp.arange(rows_dev, dtype=jnp.int32) // block_rows)[
        :, None
    ]
    variance = prior_variance
    for step in range(steps_all):
        current = block_index[0] + step
        owner_row = current // blocks_dev
        offset = current % blocks_dev * block_rows
        pending = lax.dynamic_slice_in_dim(working, offset, block_rows, 0)
        solved_here = jnp.dot(
            diag_inverse[step],
            pending,
            precision=lax.Precision.HIGHEST,
            preferred_element_type=jnp.float32,
        )
        solved = spread(solved_here.astype(jnp.bfloat16), "row", owner_row).astype(
            solved_here.dtype
        )
        variance = variance - jnp.sum(solved * solved, axis=0)
        solved_half = solved.astype(jnp.bfloat16)
        column = local_factor[:, step * block_rows : (step + 1) * block_rows]
        update = jnp.dot(
            lax.all_gather(column, "cand", axis=0, tiled=True),
            solved_half,
            preferred_element_type=jnp.float32,
        )
        working = jnp.where(global_block > current, working - update, working)
        inserted = lax.dynamic_update_slice_in_dim(working, solved, offset, 0)
        working = jnp.where(owner_row == row_here, inserted, working)
    return (working.astype(jnp.bfloat16), variance)


def solution(mesh):
    return jax.shard_map(
        shards,
        mesh=mesh,
        in_specs=(P("row", "cand"), P("row", "cand", None), P(), P("cand"), P()),
        out_specs=(P("row", "cand"), P("cand")),
        check_vma=False,
    )
```

profile of v0, /device:TPU:0, one launch (start us, length us, event | category | flops | bytes accessed | tf_op | source)
XLA Modules:
  0.0 182.9 jit_solution(3516371215284145339)
XLA Ops:
  8.0 0.0 copy-start.2
  8.0 0.0 all-reduce.3.cloned.1.call-start
  8.8 4.7 %fusion.10 = bf16[512,1024]{0,1:T(8,128)(2,1)} fusion(f32[2,512,512]{2,1,0:T(8,128)} %param.7, bf16[4096,1024]{1,0:T(8,128)(2,1)} %param.5, s32[]{:T(128)S(6)} %select_n.91, pred[]{:T(512)S(6)} %eq.15), kind=kOutput, calls=%fused_computation.15 | convolution fusion | flops 3222274048 | bytes 3145733 | tf_op jit(solution)/shard_map/dot_general | solution.py:29
  13.5 0.0 all-reduce.3.cloned.1.call-update
  13.6 0.0 all-gather.3.cloned.1.call-start
  13.6 0.0 copy-done.2
  13.6 1.1 fusion.30
  14.7 0.0 all-gather.3.cloned.1.call-update
  14.7 0.0 all-gather.5.cloned.1.call-start
  14.8 0.5 all-gather.5.cloned.1.call-update
  15.3 0.2 all-reduce.5.cloned.1.call-start
  15.6 12.0 %copy.7 = bf16[4096,1024]{0,1:T(8,128)(2,1)} copy(bf16[4096,1024]{1,0:T(8,128)(2,1)} %param.5) | data formatting | bytes 16777216 | tf_op args[0]
  27.6 40.7 %all-reduce.3.cloned.1.call-done = bf16[512,1024]{0,1:T(8,128)(2,1)} async-done(((bf16[512,1024]{0,1:T(8,128)(2,1)}), bf16[512,1024]{0,1:T(8,128)(2,1)}) %all-reduce.3.cloned.1.call-update) | async-done | bytes 1048592 | tf_op jit(solution)/shard_map/psum | solution.py:9
  68.2 0.0 copy-start.1
  68.2 0.0 all-gather.3.cloned.1.call-done
  68.2 15.8 %subtract_select_fusion.1 = f32[4096,1024]{0,1:T(8,128)} fusion(bf16[4096,1024]{0,1:T(8,128)(2,1)} %copy.7, bf16[512,1024]{0,1:T(8,128)(2,1)} %all-reduce.3.cloned.1.call-done, bf16[4096,512]{1,0:T(8,128)(2,1)} %all-gather.3.cloned.1.call-done, pred[4096]{0:T(1024)(128)(4,1)S(1)} %fusion.25), kind=kOutput, calls=%fused_computation.1 | convolution fusion | flops 4307550208 | bytes 30412800 | tf_op jit(solution)/shard_map/dot_general | solution.py:41
  84.1 0.0 copy-done.1
  84.1 0.0 copy-start.3
  84.1 3.4 %fusion.1 = (f32[1024]{0:T(1024)S(1)}, f32[4096,1024]{0,1:T(8,128)}) fusion(bf16[512,1024]{0,1:T(8,128)(2,1)S(1)} %copy-done.1, f32[4096,1024]{0,1:T(8,128)} %subtract_select_fusion.1, s32[]{:T(128)S(6)} %select_n.91, pred[]{:T(512)S(6)} %eq.16), kind=kLoop, calls=%fused_computation.7 | loop fusion | flops 2096128 | bytes 5246981 | tf_op jit(solution)/shard_map/reduce_sum | solution.py:38
  87.5 0.0 copy-done.3
  87.5 6.0 %fusion.14 = bf16[512,1024]{0,1:T(8,128)(2,1)} fusion(f32[4096,1024]{0,1:T(8,128)} %get-tuple-element.5, s32[]{:T(128)S(6)} %select_n.102, f32[2,512,512]{2,1,0:T(8,128)S(1)} %copy-done.3, pred[]{:T(512)S(6)} %eq.17), kind=kOutput, calls=%fused_computation.17 | convolution fusion | flops 3222274048 | bytes 4194309 | tf_op jit(solution)/shard_map/dot_general | solution.py:29
  93.5 0.0 all-reduce.5.cloned.1.call-update
  93.6 0.1 all-gather.5.cloned.1.call-done
  93.7 51.2 %all-reduce.5.cloned.1.call-done = bf16[512,1024]{0,1:T(8,128)(2,1)} async-done(((bf16[512,1024]{0,1:T(8,128)(2,1)}), bf16[512,1024]{0,1:T(8,128)(2,1)}) %all-reduce.5.cloned.1.call-update) | async-done | bytes 1048592 | tf_op jit(solution)/shard_map/psum | solution.py:9
  144.9 0.0 copy-start
  144.9 15.2 %subtract_select_fusion = bf16[4096,1024]{0,1:T(8,128)(2,1)} fusion(f32[4096,1024]{0,1:T(8,128)} %get-tuple-element.5, bf16[512,1024]{0,1:T(8,128)(2,1)} %all-reduce.5.cloned.1.call-done, bf16[4096,512]{1,0:T(8,128)(2,1)} %all-gather.5.cloned.1.call-done, pred[4096]{0:T(1024)(128)(4,1)S(1)} %fusion.26), kind=kOutput, calls=%fused_computation | convolution fusion | flops 4303355904 | bytes 30412800 | tf_op jit(solution)/shard_map/dot_general | solution.py:41
  160.1 0.0 copy-done
  160.1 2.6 %fusion.2 = bf16[4096,1024]{0,1:T(8,128)(2,1)} fusion(bf16[4096,1024]{0,1:T(8,128)(2,1)} %subtract_select_fusion, s32[]{:T(128)S(6)} %select_n.102, bf16[512,1024]{0,1:T(8,128)(2,1)S(1)} %copy-done, pred[]{:T(512)S(6)} %eq.18), kind=kLoop, calls=%fused_computation.8 | loop fusion | flops 1048576 | bytes 3145733 | tf_op jit(solution)/shard_map/jit(_where)/select_n | solution.py:48
  162.7 0.0 copy-start.4
  162.7 11.9 %copy.8 = bf16[4096,1024]{1,0:T(8,128)(2,1)} copy(bf16[4096,1024]{0,1:T(8,128)(2,1)} %fusion.2) | data formatting | bytes 16777216
  174.6 0.3 fusion.3
  174.9 0.0 copy-done.4
  174.9 0.6 subtract_subtract_fusion
  (2 shorter events, 0.0 us)
Async XLA Ops:
  8.0 5.6 %copy-start.2 = (bf16[1,512,1024]{2,1,0:T(8,128)(2,1)S(1)}, bf16[1,512,1024]{2,1,0:T(8,128)(2,1)}, u32[]{:S(2)}) copy-start(bf16[1,512,1024]{2,1,0:T(8,128)(2,1)} %param.6) | copy-start | bytes 3145732
  8.0 60.2 %all-reduce.3.cloned.1.call-start = ((), (), s32[]{:S(2)}) async-start(), calls=%async_computation | async-start | bytes 2097152 | tf_op jit(solution)/shard_map/psum | solution.py:9
  13.6 54.7 %all-gather.3.cloned.1.call-start = ((), (), s32[]{:S(2)}) async-start(), calls=%async_computation.1 | async-start | bytes 4718592 | tf_op jit(solution)/shard_map/all_gather | solution.py:42
  14.7 79.0 %all-gather.5.cloned.1.call-start = ((), (), s32[]{:S(2)}) async-start(), calls=%async_computation.3 | async-start | bytes 4718592 | tf_op jit(solution)/shard_map/all_gather | solution.py:42
  15.3 129.6 %all-reduce.5.cloned.1.call-start = ((), (), s32[]{:S(2)}) async-start(), calls=%async_computation.2 | async-start | bytes 2097152 | tf_op jit(solution)/shard_map/psum | solution.py:9
  68.2 15.8 %copy-start.1 = (bf16[512,1024]{0,1:T(8,128)(2,1)S(1)}, bf16[512,1024]{0,1:T(8,128)(2,1)}, u32[]{:S(2)}) copy-start(bf16[512,1024]{0,1:T(8,128)(2,1)} %all-reduce.3.cloned.1.call-done) | copy-start | bytes 3145732
  84.1 3.4 %copy-start.3 = (f32[2,512,512]{2,1,0:T(8,128)S(1)}, f32[2,512,512]{2,1,0:T(8,128)}, u32[]{:S(2)}) copy-start(f32[2,512,512]{2,1,0:T(8,128)} %param.7) | copy-start | bytes 6291460
  144.9 15.2 %copy-start = (bf16[512,1024]{0,1:T(8,128)(2,1)S(1)}, bf16[512,1024]{0,1:T(8,128)(2,1)}, u32[]{:S(2)}) copy-start(bf16[512,1024]{0,1:T(8,128)(2,1)} %all-reduce.5.cloned.1.call-done) | copy-start | bytes 3145732
  162.7 12.2 %copy-start.4 = (f32[1024]{0:T(1024)S(1)}, f32[1024]{0:T(1024)}, u32[]{:S(2)}) copy-start(f32[1024]{0:T(1024)} %param.8) | copy-start | bytes 12292
Sparse Core Ops, SparseCore 0:
  13.7 54.5 all-reduce.2
  93.7 51.1 all-reduce.4
Sparse Core Ops, SparseCore 1:
  16.1 39.2 all-gather.2
  57.1 36.5 all-gather.4
where the time goes:
time: 184 us; the launch traced here: 183 us
  waiting for transfers between devices  92.6 us (50%)
  matrix products  41.8 us (23%)
  local copies, waits for them, and re-layouts  25 us (14%)
  between operations  16.3 us (9%)
  other arithmetic  6.83 us (4%)
    psum x2, waiting for transfers between devices, spread(): return lax.psum(jnp.where(mine, value, jnp.zeros_like(value)), axis)  91.9 us
    dot_general x2, matrix products, shards(): jnp.dot(lax.all_gather(column, 'cand', axis=0, tiled=True), solved_half,...  31.1 us
    unnamed x12, local copies, waits for them, and re-layouts  24 us
    dot_general x2, matrix products, shards(): jnp.dot(diag_inverse[step], pending, precision=lax.Precision.HIGHEST, pre...  10.8 us
  transfers between devices with their start and end apart: 4, of which 3 were waited for; matrix products, arithmetic and copies ran while one was open for 21% of the time, Pallas kernels for 0%

commit v1 on v0

v1 whole, which is shorter than its diff:
```python
import functools

import jax
import jax.numpy as jnp
from jax import lax
from jax.experimental import pallas as pl
from jax.experimental.pallas import tpu as pltpu
from jax.sharding import PartitionSpec as P

MESH = pl.DeviceIdType.MESH
HALVES = 2


def bits_of(value):
    return [1 << b for b in range(value.bit_length()) if value >> b & 1]


def last_hop(rel, half):
    bits = bits_of(rel)
    if rel & 1 or half:
        return bits[0]
    return bits[-1]


def kernel(
    n_cand,
    n_row,
    chunk,
    right_ref,
    factor_ref,
    diag_ref,
    prior_ref,
    index_ref,
    out_ref,
    var_ref,
    rows_buf,
    fac_first,
    fac_second,
    out_buf,
    solved,
    arrived,
    diag_f32,
    diag_hi,
    diag_lo,
    level,
    cross,
    square,
    square_in,
    load_sem,
    store_sem,
    f_send,
    f_recv,
    z_send,
    z_recv,
    v_send,
    v_recv,
):
    fac = (fac_first, fac_second)
    rows_dev = rows_buf.shape[0]
    steps, blk = diag_f32.shape[0], diag_f32.shape[1]
    blocks_dev = rows_dev // blk
    n_chunk = solved.shape[1]
    own_rows = factor_ref.shape[1]
    half_rows = own_rows // 2
    z_rows = blk // HALVES
    me = lax.axis_index("cand")
    row = lax.axis_index("row")
    dims = [1 << b for b in range((n_cand - 1).bit_length())]

    def device_at(rel):
        return me + sum(b * (1 - 2 * ((me // b) % 2)) for b in bits_of(rel))

    load_rows = pltpu.make_async_copy(right_ref, rows_buf, load_sem.at[0])
    load_diag = pltpu.make_async_copy(diag_ref, diag_f32, load_sem.at[1])
    load_diag.start()
    load_rows.start()
    own_copies = []
    for s in range(steps):
        cp = pltpu.make_async_copy(
            factor_ref.at[0, :, pl.ds(s * blk, blk)],
            fac[s].at[pl.ds(pl.multiple_of(me * own_rows, own_rows), own_rows)],
            load_sem.at[2 + s],
        )
        cp.start()
        own_copies.append(cp)

    barrier = pltpu.get_barrier_semaphore()
    for d in dims:
        pl.semaphore_signal(barrier, inc=1, device_id=(device_at(d), row), device_id_type=MESH)
    for k in range(1, n_row):
        other = lax.rem(row + k, n_row)
        pl.semaphore_signal(barrier, inc=1, device_id=(me, other), device_id_type=MESH)
    pl.semaphore_wait(barrier, len(dims) + n_row - 1)

    def piece_rows(rel, half):
        start = device_at(rel) * own_rows + half * half_rows
        return pl.ds(pl.multiple_of(start, half_rows), half_rows)

    def f_copy(s, rel, half):
        dim = last_hop(rel, half)
        held = rel ^ dim
        dst = fac[s].at[piece_rows(held, half)]
        if held == 0:
            src = factor_ref.at[0, pl.ds(half * half_rows, half_rows), pl.ds(s * blk, blk)]
        else:
            src = dst
        return pltpu.make_async_remote_copy(
            src_ref=src,
            dst_ref=dst,
            send_sem=f_send.at[s, rel, half],
            recv_sem=f_recv.at[s, rel, half],
            device_id=(device_at(dim), row),
            device_id_type=MESH,
        )

    def f_arrival(s, rel, half):
        dim = last_hop(rel, half)
        dst = fac[s].at[piece_rows(rel, half)]
        return pltpu.make_async_remote_copy(
            src_ref=dst,
            dst_ref=dst,
            send_sem=f_send.at[s, rel, half],
            recv_sem=f_recv.at[s, rel, half],
            device_id=(device_at(dim), row),
            device_id_type=MESH,
        )

    def f_start_own(s):
        for turn in range(2):
            for i, d in enumerate(reversed(dims)):
                half = turn if d == 2 or d == 1 else 1 - turn
                f_copy(s, d, half).start()

    forwards = [
        (rel, half)
        for rel in range(1, n_cand)
        if len(bits_of(rel)) > 1
        for half in range(2)
    ]

    def f_pass_on(s, rel, half):
        f_arrival(s, rel, half).wait_recv()
        nexts = [q for q, h in forwards if h == half and q ^ last_hop(q, h) == rel]
        for q in sorted(nexts, key=lambda q: q & 1):
            f_copy(s, q, half).start()

    singles = [d for d in dims if d > 1]
    waited = {(d, h) for d in singles for h in range(2)}

    def f_action(s, number):
        if number == 0:
            for d in singles:
                f_pass_on(s, d, 0 if d == 2 else 1)
        elif number == 1:
            for d in singles:
                f_pass_on(s, d, 1 if d == 2 else 0)
        elif number == 2:
            relays = [q for q in range(2, n_cand, 2) if len(bits_of(q)) > 1]
            for q in sorted(relays, key=lambda q: len(bits_of(q))):
                for half in range(2):
                    waited.add((q, half))
                    f_pass_on(s, q, half)
        else:
            for rel in range(1, n_cand):
                for half in range(2):
                    if (rel, half) not in waited:
                        f_arrival(s, rel, half).wait_recv()

    f_start_own(0)

    place = jnp.clip(index_ref[0] - row * blocks_dev, -2, blocks_dev).astype(jnp.float32)
    level[...] = jnp.full(level.shape, place).astype(jnp.bfloat16)

    def at(width):
        return level[:, :width]

    def own(s, value, other):
        here = level[: value.shape[0], : value.shape[1]].astype(value.dtype)
        inside = jnp.where(here < blocks_dev - s, value, other)
        return jnp.where(here >= -s, inside, other)

    def block_of(ref, s, cols):
        value = ref[:blk, cols]
        for b in range(1, blocks_dev):
            value = jnp.where(at(value.shape[1]) == b - s, ref[b * blk : (b + 1) * blk, cols], value)
        return value

    def z_copy(s, j, half):
        part = pl.ds(half * z_rows, z_rows)
        return pltpu.make_async_remote_copy(
            src_ref=solved.at[s, j, part],
            dst_ref=arrived.at[s, j, part],
            send_sem=z_send.at[s, j, half],
            recv_sem=z_recv.at[s, j, half],
            device_id=(me, lax.rem(row + 1, n_row)),
            device_id_type=MESH,
        )

    def z_send_on(s, j, half):
        @pl.when(row < n_row - 1)
        def _():
            z_copy(s, j, half).start()

    def z_take(s, j, half):
        part = pl.ds(half * z_rows, z_rows)

        @pl.when(row > 0)
        def _():
            z_copy(s, j, half).wait_recv()
            solved[s, j, part, :] = own(s, solved[s, j, part, :], arrived[s, j, part, :])

    def dot(a, b):
        return jnp.dot(a, b, preferred_element_type=jnp.float32)

    def add_squares(s, j, value):
        sums = jnp.sum((value * value).reshape(blk // 8, 8, chunk), axis=0)
        square[j] = square[j] + own(s, sums, jnp.zeros_like(sums))

    load_diag.wait()
    for s in range(steps):
        full = diag_f32[s]
        high = full.astype(jnp.bfloat16)
        diag_hi[s] = high
        diag_lo[s] = (full - high.astype(jnp.float32)).astype(jnp.bfloat16)
    square[...] = jnp.zeros_like(square)
    load_rows.wait()

    def columns(j):
        return slice(j * chunk, (j + 1) * chunk)

    for j in range(n_chunk):
        pending = block_of(rows_buf, 0, columns(j))
        value = dot(diag_hi[0], pending) + dot(diag_lo[0], pending)
        solved[0, j] = value.astype(jnp.bfloat16)
        add_squares(0, j, value)

        @pl.when(row == 0)
        def _():
            for half in range(HALVES):
                z_copy(0, j, half).start()

    for cp in own_copies:
        cp.wait()

    def z_later(s, j, half):
        @pl.when(jnp.logical_and(row > 0, row < n_row - 1))
        def _():
            z_copy(s, j, half).start()

    z_units = n_chunk * HALVES

    for k in range(z_units):
        j, half = k // HALVES, k % HALVES
        z_take(0, j, half)
        z_later(0, j, half)
        if k == 0:
            f_action(0, 0)
        if k == z_units // 4:
            f_action(0, 1)
            f_start_own(1)
        if k == z_units // 2:
            f_action(0, 2)
    f_action(0, 3)
    cross[...] = block_of(fac[0], 1, slice(0, blk))

    def candidate(s, j):
        update = dot(cross[...], solved[0, j])
        pending = block_of(rows_buf, s, columns(j)).astype(jnp.float32) - update
        high = pending.astype(jnp.bfloat16)
        low = (pending - high.astype(jnp.float32)).astype(jnp.bfloat16)
        value = dot(diag_hi[s], high) + (dot(diag_lo[s], high) + dot(diag_hi[s], low))
        solved[s, j] = value.astype(jnp.bfloat16)
        add_squares(s, j, value)

    def finish(j):
        def body(b, _):
            rows = pl.ds(pl.multiple_of(b * blk, blk), blk)
            below = jnp.full((blk, chunk), b.astype(jnp.float32)).astype(jnp.bfloat16) - at(chunk)
            base = rows_buf[rows, columns(j)]
            update = dot(fac[0][rows, :], solved[0, j]) + dot(fac[1][rows, :], solved[1, j])
            moved = (base.astype(jnp.float32) - update).astype(jnp.bfloat16)
            value = jnp.where(below > 1, moved, base)
            value = jnp.where(below == 0, solved[0, j], value)
            value = jnp.where(below == 1, solved[1, j], value)
            out_buf[rows, columns(j)] = value
            return 0

        for part in range(2):
            lax.fori_loop(part * blocks_dev // 2, (part + 1) * blocks_dev // 2, body, 0)
            store(j, part).start()

    def store(j, part):
        rows = pl.ds(part * rows_dev // 2, rows_dev // 2)
        cols = pl.ds(j * chunk, chunk)
        return pltpu.make_async_copy(
            out_buf.at[rows, cols], out_ref.at[rows, cols], store_sem.at[j, part]
        )

    def v_copy(k):
        return pltpu.make_async_remote_copy(
            src_ref=square,
            dst_ref=square_in.at[k - 1],
            send_sem=v_send.at[k - 1],
            recv_sem=v_recv.at[k - 1],
            device_id=(me, lax.rem(row + k, n_row)),
            device_id_type=MESH,
        )

    done = 0
    for k in range(z_units):
        j, half = k // HALVES, k % HALVES
        if half == 0:
            candidate(1, j)
        z_take(1, j, half)
        z_send_on(1, j, half)
        if k == 0:
            f_action(1, 0)
        if k == z_units // 8:
            f_action(1, 1)
        if k == 3 * z_units // 8:
            f_action(1, 2)
        if k == z_units // 2:
            f_action(1, 3)
        if k == z_units - HALVES:
            for other in range(1, n_row):
                v_copy(other).start()
        if k >= z_units // 2:
            while done < j and done <= k - z_units // 2:
                finish(done)
                done += 1
    while done < n_chunk:
        finish(done)
        done += 1

    total = square[...]
    for other in range(1, n_row):
        v_copy(other).wait_recv()
        total = total + square_in[other - 1]
    for j in range(n_chunk):
        var_ref[:, columns(j)] = prior_ref[:, columns(j)] - jnp.sum(total[j], axis=0, keepdims=True)

    for s in range(steps):
        for rel in range(1, n_cand):
            for half in range(2):
                f_copy(s, rel, half).wait_send()

    @pl.when(row < n_row - 1)
    def _():
        for s in range(steps):
            for k in range(z_units):
                z_copy(s, k // HALVES, k % HALVES).wait_send()

    for other in range(1, n_row):
        v_copy(other).wait_send()
    for j in range(n_chunk):
        for part in range(2):
            store(j, part).wait()


def shards(n_cand, n_row, right_side, factor_panel, diag_inverse, prior_variance, block_index):
    rows_dev, cands = right_side.shape
    steps, blk = diag_inverse.shape[:2]
    chunk = 256
    n_chunk = cands // chunk
    bf16, f32 = jnp.bfloat16, jnp.float32
    any_space = pl.BlockSpec(memory_space=pl.ANY)
    vmem = pl.BlockSpec(memory_space=pltpu.VMEM)
    dma = pltpu.SemaphoreType.DMA
    out, variance = pl.pallas_call(
        functools.partial(kernel, n_cand, n_row, chunk),
        out_shape=(
            jax.ShapeDtypeStruct((rows_dev, cands), bf16),
            jax.ShapeDtypeStruct((1, cands), f32),
        ),
        in_specs=[any_space, any_space, any_space, vmem, pl.BlockSpec(memory_space=pltpu.SMEM)],
        out_specs=(any_space, vmem),
        scratch_shapes=[
            pltpu.VMEM((rows_dev, cands), bf16),
            pltpu.VMEM((rows_dev, blk), bf16),
            pltpu.VMEM((rows_dev, blk), bf16),
            pltpu.VMEM((rows_dev, cands), bf16),
            pltpu.VMEM((steps, n_chunk, blk, chunk), bf16),
            pltpu.VMEM((steps, n_chunk, blk, chunk), bf16),
            pltpu.VMEM((steps, blk, blk), f32),
            pltpu.VMEM((steps, blk, blk), bf16),
            pltpu.VMEM((steps, blk, blk), bf16),
            pltpu.VMEM((blk, blk), bf16),
            pltpu.VMEM((blk, blk), bf16),
            pltpu.VMEM((n_chunk, 8, chunk), f32),
            pltpu.VMEM((n_row - 1, n_chunk, 8, chunk), f32),
            dma((2 + steps,)),
            dma((n_chunk, 2)),
            dma((steps, n_cand, 2)),
            dma((steps, n_cand, 2)),
            dma((steps, n_chunk, HALVES)),
            dma((steps, n_chunk, HALVES)),
            dma((n_row - 1,)),
            dma((n_row - 1,)),
        ],
        compiler_params=pltpu.CompilerParams(
            collective_id=0, has_side_effects=True, vmem_limit_bytes=56 << 20
        ),
        cost_estimate=pl.CostEstimate(
            flops=2 * rows_dev * cands * steps * blk, bytes_accessed=32 << 20, transcendentals=0
        ),
        name="block_steps",
    )(right_side, factor_panel, diag_inverse, prior_variance.reshape(1, cands), block_index)
    return out, variance.reshape(cands)


def solution(mesh):
    return jax.shard_map(
        functools.partial(shards, mesh.shape["cand"], mesh.shape["row"]),
        mesh=mesh,
        in_specs=(P("row", "cand"), P("row", "cand", None), P(), P("cand"), P()),
        out_specs=(P("row", "cand"), P("cand")),
        check_vma=False,
    )
```

time: 184 us -> 83.4 us (0.45)
  waiting for transfers between devices: 92.6 us -> 0 us
  Pallas kernels: 0 us -> 72.3 us
  matrix products: 41.8 us -> 0 us
  local copies, waits for them, and re-layouts: 25 us -> 8.36 us
  between operations: 16.3 us -> 1.29 us
  other arithmetic: 6.83 us -> 0 us
    psum x2 -> x0, waiting for transfers between devices: 91.9 us -> none  [spread(): return lax.psum(jnp.where(mine, value, jnp.zeros_like(value)), axis)]
    pallas_call x0 -> x1, Pallas kernels: none -> 72.3 us  [shards(): pl.pallas_call(functools.partial(kernel, n_cand, n_row, chunk), out_shape...]
    dot_general x4 -> x0, matrix products: 41.8 us -> none  [the longest x2 31.1 us: shards(): jnp.dot(lax.all_gather(column, 'cand', axis=0, tiled=True), solved_half,...]
    unnamed x12 -> x4, local copies, waits for them, and re-layouts: 24 us -> 8.36 us
    reduce_sum x2 -> x0, other arithmetic: 3.65 us -> none  [shards(): variance = variance - jnp.sum(solved * solved, axis=0)]
    select_n x1 -> x0, other arithmetic: 2.56 us -> none  [shards(): working = jnp.where(owner_row == row_here, inserted, working)]
  transfers between devices with their start and end apart: 4 -> 0, of which waited for: 3 -> 0; matrix products, arithmetic and copies ran while one was open for 21% -> 0% of each run, Pallas kernels for 0% -> 0%
where the time goes in v1:
time: 83.4 us; the launch traced here: 82 us
  Pallas kernels  72.3 us (87%)
  local copies, waits for them, and re-layouts  8.36 us (10%)
  between operations  1.29 us (2%)
    pallas_call x1, Pallas kernels, shards(): pl.pallas_call(functools.partial(kernel, n_cand, n_row, chunk), out_shape...  72.3 us
    unnamed x4, local copies, waits for them, and re-layouts  8.36 us

profile of v1, /device:TPU:0, one launch (start us, length us, event | category | flops | bytes accessed | tf_op | source)
XLA Modules:
  0.0 82.0 jit_solution(14945671620810357636)
XLA Ops:
  1.3 72.3 %block_steps.1 = (bf16[4096,1024]{1,0:T(8,128)(2,1)}, f32[1,1024]{1,0:T(1,128)}) custom-call(bf16[4096,1024]{1,0:T(8,128)(2,1)} %right_ref.1, bf16[1,512,1024]{2,1,0:T(8,128)(2,1)} %factor_ref.1, f32[2,512,512]{2,1,0:T(8,128)} %diag_ref.1, f32[1,1024]{1,0:T(1,128)} %bitcast.3, s32[1]{0:T(128)S(6)} %copy.9.index_ref), custom_call_target="tpu_custom_call" | custom-call | flops 8589934592 | bytes 33554432 | tf_op jit(solution)/shard_map/block_steps/pallas_call | solution.py:369
  73.6 0.0 copy-start
  73.6 7.8 %copy.10 = bf16[4096,1024]{1,0:T(8,128)(2,1)} copy(bf16[4096,1024]{1,0:T(8,128)(2,1)} %get-tuple-element.8) | data formatting | bytes 16777216
  81.4 0.0 copy-done
  81.4 0.6 copy.11
Async XLA Ops:
  73.6 7.8 %copy-start = (f32[1,1024]{1,0:T(1,128)S(1)}, f32[1,1024]{1,0:T(1,128)}, u32[]{:S(2)}) copy-start(f32[1,1024]{1,0:T(1,128)} %get-tuple-element.5) | copy-start | bytes 12292

commit v2 on v1

--- a/solution.py
+++ b/solution.py
@@ -36,7 +36,6 @@
     rows_buf,
     fac_first,
     fac_second,
-    out_buf,
     solved,
     arrived,
     diag_f32,
@@ -47,7 +46,6 @@
     square,
     square_in,
     load_sem,
-    store_sem,
     f_send,
     f_recv,
     z_send,
@@ -216,12 +214,14 @@
         sums = jnp.sum((value * value).reshape(blk // 8, 8, chunk), axis=0)
         square[j] = square[j] + own(s, sums, jnp.zeros_like(sums))
 
-    load_diag.wait()
-    for s in range(steps):
+    def split_diag(s):
         full = diag_f32[s]
         high = full.astype(jnp.bfloat16)
         diag_hi[s] = high
         diag_lo[s] = (full - high.astype(jnp.float32)).astype(jnp.bfloat16)
+
+    load_diag.wait()
+    split_diag(0)
     square[...] = jnp.zeros_like(square)
     load_rows.wait()
 
@@ -239,6 +239,7 @@
             for half in range(HALVES):
                 z_copy(0, j, half).start()
 
+    split_diag(1)
     for cp in own_copies:
         cp.wait()
 
@@ -282,19 +283,11 @@
             value = jnp.where(below > 1, moved, base)
             value = jnp.where(below == 0, solved[0, j], value)
             value = jnp.where(below == 1, solved[1, j], value)
-            out_buf[rows, columns(j)] = value
+            out_ref[rows, columns(j)] = value
             return 0
 
         for part in range(2):
             lax.fori_loop(part * blocks_dev // 2, (part + 1) * blocks_dev // 2, body, 0)
-            store(j, part).start()
-
-    def store(j, part):
-        rows = pl.ds(part * rows_dev // 2, rows_dev // 2)
-        cols = pl.ds(j * chunk, chunk)
-        return pltpu.make_async_copy(
-            out_buf.at[rows, cols], out_ref.at[rows, cols], store_sem.at[j, part]
-        )
 
     def v_copy(k):
         return pltpu.make_async_remote_copy(
@@ -352,9 +345,21 @@
 
     for other in range(1, n_row):
         v_copy(other).wait_send()
-    for j in range(n_chunk):
-        for part in range(2):
-            store(j, part).wait()
+
+
+def write_kernel(src_ref, dst_ref, sems):
+    parts = sems.shape[0]
+    rows = src_ref.shape[0] // parts
+    copies = [
+        pltpu.make_async_copy(
+            src_ref.at[pl.ds(p * rows, rows)], dst_ref.at[pl.ds(p * rows, rows)], sems.at[p]
+        )
+        for p in range(parts)
+    ]
+    for cp in copies:
+        cp.start()
+    for cp in copies:
+        cp.wait()
 
 
 def shards(n_cand, n_row, right_side, factor_panel, diag_inverse, prior_variance, block_index):
@@ -373,12 +378,11 @@
             jax.ShapeDtypeStruct((1, cands), f32),
         ),
         in_specs=[any_space, any_space, any_space, vmem, pl.BlockSpec(memory_space=pltpu.SMEM)],
-        out_specs=(any_space, vmem),
+        out_specs=(vmem, vmem),
         scratch_shapes=[
             pltpu.VMEM((rows_dev, cands), bf16),
             pltpu.VMEM((rows_dev, blk), bf16),
             pltpu.VMEM((rows_dev, blk), bf16),
-            pltpu.VMEM((rows_dev, cands), bf16),
             pltpu.VMEM((steps, n_chunk, blk, chunk), bf16),
             pltpu.VMEM((steps, n_chunk, blk, chunk), bf16),
             pltpu.VMEM((steps, blk, blk), f32),
@@ -389,7 +393,6 @@
             pltpu.VMEM((n_chunk, 8, chunk), f32),
             pltpu.VMEM((n_row - 1, n_chunk, 8, chunk), f32),
             dma((2 + steps,)),
-            dma((n_chunk, 2)),
             dma((steps, n_cand, 2)),
             dma((steps, n_cand, 2)),
             dma((steps, n_chunk, HALVES)),
@@ -398,14 +401,23 @@
             dma((n_row - 1,)),
         ],
         compiler_params=pltpu.CompilerParams(
-            collective_id=0, has_side_effects=True, vmem_limit_bytes=56 << 20
+            collective_id=0, has_side_effects=True, vmem_limit_bytes=42 << 20
         ),
         cost_estimate=pl.CostEstimate(
             flops=2 * rows_dev * cands * steps * blk, bytes_accessed=32 << 20, transcendentals=0
         ),
         name="block_steps",
     )(right_side, factor_panel, diag_inverse, prior_variance.reshape(1, cands), block_index)
-    return out, variance.reshape(cands)
+    written = pl.pallas_call(
+        write_kernel,
+        out_shape=jax.ShapeDtypeStruct(out.shape, out.dtype),
+        in_specs=[any_space],
+        out_specs=any_space,
+        scratch_shapes=[dma((4,))],
+        compiler_params=pltpu.CompilerParams(vmem_limit_bytes=4 << 20),
+        name="write_rows",
+    )(out)
+    return written, variance.reshape(cands)
 
 
 def solution(mesh):

time: 83.4 us -> 80.3 us (0.963); the launches traced: 82 us -> 79.8 us
  local copies, waits for them, and re-layouts: 8.36 us -> 4.09 us
  Pallas kernels: 72.3 us -> 74.4 us
    unnamed x4 -> x7, local copies, waits for them, and re-layouts: 8.36 us -> 4.09 us
    pallas_call x0 -> x1, Pallas kernels: none -> 3.37 us  [shards(): pl.pallas_call(write_kernel, out_shape=jax.ShapeDtypeStruct(out.shape, ou...]
    pallas_call x1, Pallas kernels: 72.3 us -> 71.1 us  [shards(): pl.pallas_call(functools.partial(kernel, n_cand, n_row, chunk), out_shape...]
where the time goes in v2:
time: 80.3 us; the launch traced here: 79.8 us
  Pallas kernels  74.4 us (93%)
  local copies, waits for them, and re-layouts  4.09 us (5%)
  between operations  1.3 us (2%)
    pallas_call x1, Pallas kernels, shards(): pl.pallas_call(functools.partial(kernel, n_cand, n_row, chunk), out_shape...  71.1 us
    unnamed x7, local copies, waits for them, and re-layouts  4.09 us
    pallas_call x1, Pallas kernels, shards(): pl.pallas_call(write_kernel, out_shape=jax.ShapeDtypeStruct(out.shape, ou...  3.37 us

profile of v2, /device:TPU:0, one launch (start us, length us, event | category | flops | bytes accessed | tf_op | source)
XLA Modules:
  0.0 79.8 jit_solution(13137880440421247693)
XLA Ops:
  1.3 0.0 copy-start
  1.3 1.6 %copy-done = f32[2,512,512]{2,1,0:T(8,128)S(1)} copy-done((f32[2,512,512]{2,1,0:T(8,128)S(1)}, f32[2,512,512]{2,1,0:T(8,128)}, u32[]{:S(2)}) %copy-start) | copy-done | bytes 2097176
  2.9 0.0 copy-start.1
  2.9 1.2 %copy-done.1 = bf16[1,512,1024]{2,1,0:T(8,128)(2,1)S(1)} copy-done((bf16[1,512,1024]{2,1,0:T(8,128)(2,1)S(1)}, bf16[1,512,1024]{2,1,0:T(8,128)(2,1)}, u32[]{:S(2)}) %copy-start.1) | copy-done | bytes 1048600
  4.1 0.0 copy-start.2
  4.1 0.7 copy-done.2
  4.8 71.1 %block_steps.1 = (bf16[4096,1024]{1,0:T(8,128)(2,1)S(1)}, f32[1,1024]{1,0:T(1,128)S(1)}) custom-call(bf16[4096,1024]{1,0:T(8,128)(2,1)} %right_ref.1, bf16[1,512,1024]{2,1,0:T(8,128)(2,1)S(1)} %copy-done.1, f32[2,512,512]{2,1,0:T(8,128)S(1)} %copy-done, f32[1,1024]{1,0:T(1,128)S(1)} %bitcast.3, s32[1]{0:T(128)S(6)} %copy.8.index_ref), custom_call_target="tpu_custom_call" | custom-call | flops 8589934592 | bytes 33554432 | tf_op jit(solution)/shard_map/block_steps/pallas_call | solution.py:374
  75.9 3.4 %write_rows.1 = bf16[4096,1024]{1,0:T(8,128)(2,1)} custom-call(bf16[4096,1024]{1,0:T(8,128)(2,1)S(1)} %get-tuple-element.4.src_ref), custom_call_target="tpu_custom_call" | custom-call | tf_op jit(solution)/shard_map/write_rows/pallas_call | solution.py:411
  79.2 0.6 copy.9
Async XLA Ops:
  1.3 1.6 %copy-start = (f32[2,512,512]{2,1,0:T(8,128)S(1)}, f32[2,512,512]{2,1,0:T(8,128)}, u32[]{:S(2)}) copy-start(f32[2,512,512]{2,1,0:T(8,128)} %diag_ref.1) | copy-start | bytes 6291460
  2.9 1.2 %copy-start.1 = (bf16[1,512,1024]{2,1,0:T(8,128)(2,1)S(1)}, bf16[1,512,1024]{2,1,0:T(8,128)(2,1)}, u32[]{:S(2)}) copy-start(bf16[1,512,1024]{2,1,0:T(8,128)(2,1)} %factor_ref.1) | copy-start | bytes 3145732
  4.1 0.7 copy-start.2
